TPU v7x, 512 devices: a whole 4x8x8 slice. The times are simulated.
512 devices in a mesh: dp: 64 (over y, x, core), tensor: 8 (over z).
Axes of the slice: x: 4, y: 8, z: 8, core: 2. Of those that a mesh axis runs over, the one named last changes fastest.
Arguments:
- features: bfloat16 [16384, 8192], P('dp', 'tensor'), may hold values from -6 to 6
- gate_pre: bfloat16 [16384, 14336], P('dp', 'tensor'), may hold values from -6 to 6
- up_pre: bfloat16 [16384, 14336], P('dp', 'tensor'), may hold values from -6 to 6
- grad_hidden: bfloat16 [16384, 14336], P('dp', 'tensor'), may hold values from -0.4375 to 0.4375
- blocks: int32 [512, 3], P('tensor'), may hold values from 0 to 63, as said below
- owner: int32 [512], P('tensor'), may hold values from 0 to 63, as said below
- weights: float32 [1536, 128, 128], P(('dp', 'tensor')), may hold values from -0.4375 to 0.4375
- moment1: float32 [1536, 128, 128], P(('dp', 'tensor')), may hold values from -6 to 6
- moment2: float32 [1536, 128, 128], P(('dp', 'tensor')), may hold values from 0.05 to 2
Outputs:
- new_weights: float32 [1536, 128, 128], P(('dp', 'tensor'))
- new_moment1: float32 [1536, 128, 128], P(('dp', 'tensor'))
- new_moment2: float32 [1536, 128, 128], P(('dp', 'tensor'))
Inputs may be any that keep to these rules, and one draw needn't show every extreme that they name: Each row is (matrix, row block, column block): matrix 0 is the gate and 1 the up projection, row block below 64, column block below 14 and counted within the tensor index's own columns. The rows of one tensor index's list are distinct; columns hold unequal numbers of blocks. `owner`: in each tensor index's list no index of dp owns more than 3 blocks, and some index of dp owns exactly 3.
All inputs are finite; a program needn't handle non-finite values.
Results may differ from a plain program's by a relative error of at most 0.0028.
Values may be sent and summed in bfloat16 or wider, within the bound.
A program may use at most 64 MiB of HBM per device.

v0:
```python
import jax
import jax.numpy as jnp
from jax import lax
from jax.sharding import PartitionSpec as P

beta_first = 0.9
beta_second = 0.999
learn_rate = 0.01
epsilon = 1e-08
bias_first = 1.0 - 0.9**10
bias_second = 1.0 - 0.999**10


def local(features, gate_pre, up_pre, grad_hidden, blocks, owner, weights, moment1, moment2):
    block_size = weights.shape[-1]
    capacity = weights.shape[0]
    replicas = lax.axis_size("dp")
    listed = owner.shape[0]
    gathered = lax.all_gather(features, "tensor", axis=1, tiled=True)
    tokens = gathered.shape[0]
    column_blocks = gate_pre.shape[1] // block_size
    gate_value = gate_pre.astype(jnp.float32)
    cotangent = grad_hidden.astype(jnp.float32)
    sigmoid_gate = jax.nn.sigmoid(gate_value)
    grad_up = (cotangent * (gate_value * sigmoid_gate)).astype(jnp.bfloat16)
    grad_gate = (
        cotangent
        * up_pre.astype(jnp.float32)
        * (sigmoid_gate * (1.0 + gate_value * (1.0 - sigmoid_gate)))
    ).astype(jnp.bfloat16)
    row_cells = gathered.reshape(tokens, -1, block_size)
    chosen_rows = jnp.take(row_cells, blocks[:, 1], axis=1)
    activations = jnp.concatenate(
        [
            grad_gate.reshape(tokens, column_blocks, block_size),
            grad_up.reshape(tokens, column_blocks, block_size),
        ],
        axis=1,
    )
    chosen_cols = jnp.take(activations, blocks[:, 0] * column_blocks + blocks[:, 2], axis=1)
    partial_value = jnp.einsum(
        "tbi,tbj->bij", chosen_rows, chosen_cols, preferred_element_type=jnp.float32
    )
    earlier = lax.broadcasted_iota(jnp.int32, (listed, listed), 1) < lax.broadcasted_iota(
        jnp.int32, (listed, listed), 0
    )
    slot_rank = jnp.sum(((owner[:, None] == owner[None, :]) & earlier).astype(jnp.int32), axis=1)
    owner_index = lax.axis_index("dp")
    target = owner * capacity + slot_rank
    outgoing = (
        jnp.zeros((replicas * capacity, block_size, block_size), jnp.float32)
        .at[target]
        .set(partial_value)
    )
    incoming = lax.all_to_all(
        outgoing.astype(jnp.bfloat16), "dp", split_axis=0, concat_axis=0, tiled=True
    ).astype(outgoing.dtype)
    block_grad = jnp.sum(incoming.reshape(replicas, capacity, block_size, block_size), axis=0)
    held_count = jnp.sum((owner == owner_index).astype(jnp.int32))
    is_valid = (jnp.arange(capacity, dtype=jnp.int32) < held_count)[:, None, None]
    first_new = beta_first * moment1 + (1.0 - beta_first) * block_grad
    second_new = beta_second * moment2 + (1.0 - beta_second) * block_grad * block_grad
    weight_new = weights - learn_rate * (first_new / bias_first) / (
        jnp.sqrt(second_new / bias_second) + epsilon
    )
    return (
        jnp.where(is_valid, weight_new, weights),
        jnp.where(is_valid, first_new, moment1),
        jnp.where(is_valid, second_new, moment2),
    )


def solution(mesh):
    placed = (
        P("dp", "tensor"),
        P("dp", "tensor"),
        P("dp", "tensor"),
        P("dp", "tensor"),
        P("tensor", None),
        P("tensor"),
        P(("dp", "tensor"), None, None),
        P(("dp", "tensor"), None, None),
        P(("dp", "tensor"), None, None),
    )
    return jax.shard_map(
        local,
        mesh=mesh,
        in_specs=placed,
        out_specs=(
            P(("dp", "tensor"), None, None),
            P(("dp", "tensor"), None, None),
            P(("dp", "tensor"), None, None),
        ),
        check_vma=False,
    )
```

profile of v0, /device:TPU:1, one launch (start us, length us, event | category | flops | bytes accessed | tf_op | source)
XLA Modules:
  0.0 280.3 jit_solution(7730852661984782400)
XLA Ops:
  7.2 0.0 copy-start
  7.2 0.0 all-gather.2.cloned.1.call-start
  7.2 2.2 copy.27
  9.4 0.0 all-gather.2.cloned.1.call-update
  9.4 1.5 copy.31
  10.9 2.2 copy.30
  13.1 0.0 copy-done
  13.1 1.3 copy.29
  14.4 2.5 fusion.9
  16.9 0.6 copy.32
  17.5 1.3 copy.33
  18.8 1.3 pad_maximum_fusion
  20.2 0.0 copy-start.5
  20.2 3.0 %gather_fusion.1 = bf16[64,256,128]{2,1,0:T(8,128)(2,1)} fusion(bf16[256,28,128]{2,0,1:T(8,128)(2,1)S(1)} %pad_maximum_fusion, s32[1024]{0:T(1024)S(1)} %pad_clamp_fusion), kind=kCustom, calls=%fused_computation.1 | custom fusion | bytes 8388864 | tf_op jit(solution)/shard_map/jit(_take)/gather | solution.py:40
  23.3 0.0 copy-done.5
  23.3 0.2 convert_reduce_fusion.1
  23.4 0.6 fusion.20
  24.1 49.8 %all-gather.2.cloned.1.call-done = bf16[256,8192]{0,1:T(8,128)(2,1)} async-done(((bf16[256,1024]{0,1:T(8,128)(2,1)}), bf16[256,8192]{0,1:T(8,128)(2,1)}) %all-gather.2.cloned.1.call-update) | async-done | bytes 4194320 | tf_op jit(solution)/shard_map/all_gather | solution.py:19
  73.9 6.3 %copy.28 = bf16[256,64,128]{2,0,1:T(8,128)(2,1)} copy(bf16[256,64,128]{0,2,1:T(8,128)(2,1)} %bitcast.19) | data formatting | bytes 8388608 | tf_op jit(solution)/shard_map/reshape | solution.py:31
  80.3 5.2 %gather_fusion = bf16[64,256,128]{2,1,0:T(8,128)(2,1)} fusion(bf16[256,64,128]{2,0,1:T(8,128)(2,1)} %copy.28, s32[1024]{0:T(1024)S(1)} %pad_clamp_fusion.1), kind=kCustom, calls=%fused_computation | custom fusion | bytes 8388864 | tf_op jit(solution)/shard_map/jit(_take)/gather | solution.py:32
  85.5 7.0 %fusion = f32[64,128,128]{2,1,0:T(8,128)} fusion(bf16[64,256,128]{2,1,0:T(8,128)(2,1)} %gather_fusion.1, bf16[64,256,128]{2,1,0:T(8,128)(2,1)} %gather_fusion, pred[64]{0:T(512)(128)(4,1)S(1)} %get-tuple-element.3, pred[64]{0:T(512)(128)(4,1)S(1)} %get-tuple-element.10), kind=kOutput, calls=%fused_computation.4 | convolution fusion | flops 541065216 | bytes 12583040 | tf_op jit(solution)/shard_map/tbi,tbj->bij/dot_general | solution.py:41
  92.5 6.1 %broadcast_in_dim.42 = f32[192,128,128]{2,1,0:T(8,128)} broadcast(f32[]{:T(128)} %constant.17.clone.1), dimensions={} | broadcast | bytes 12582916 | tf_op jit(solution)/shard_map/broadcast_in_dim | solution.py:51
  98.6 12.1 %scatter_fusion = f32[192,128,128]{2,1,0:T(8,128)} fusion(f32[192,128,128]{2,1,0:T(8,128)} %broadcast_in_dim.42, s32[64]{0:T(128)S(1)} %get-tuple-element.12, f32[64,128,128]{2,1,0:T(8,128)} %fusion), kind=kCustom, calls=%fused_computation.2 | custom fusion | bytes 12583168 | tf_op jit(solution)/shard_map/scatter | solution.py:53
  110.7 8.8 %convert_element_type.32 = bf16[192,128,128]{2,1,0:T(8,128)(2,1)} convert(f32[192,128,128]{2,1,0:T(8,128)} %scatter_fusion) | non-fusion elementwise | flops 3145728 | bytes 18874368 | tf_op jit(solution)/shard_map/convert_element_type | solution.py:56
  119.4 10.5 %all-to-all-start = ((bf16[192,128,128]{2,1,0:T(8,128)(2,1)}), bf16[192,128,128]{2,1,0:T(8,128)(2,1)}, u32[]{:S(2)}, u32[]{:S(2)}) async-start(bf16[192,128,128]{2,1,0:T(8,128)(2,1)} %convert_element_type.32), calls=%async_computation | async-start | bytes 12582912 | tf_op jit(solution)/shard_map/all_to_all | solution.py:55
  130.0 0.0 copy-start.1
  130.0 0.0 copy-start.2
  130.0 0.0 copy-start.3
  130.0 0.7 iota_compare_fusion.1
  130.7 137.8 %all-to-all-done = bf16[192,128,128]{2,1,0:T(8,128)(2,1)} async-done(((bf16[192,128,128]{2,1,0:T(8,128)(2,1)}), bf16[192,128,128]{2,1,0:T(8,128)(2,1)}, u32[]{:S(2)}, u32[]{:S(2)}) %all-to-all-start) | async-done | bytes 6291488 | tf_op jit(solution)/shard_map/all_to_all | solution.py:55
  268.5 3.9 %convert_reduce_fusion = f32[3,128,128]{2,1,0:T(8,128)S(1)} fusion(bf16[64,3,128,128]{3,2,1,0:T(8,128)(2,1)} %bitcast.10), kind=kLoop, calls=%fused_computation.3 | loop fusion | flops 6242304 | bytes 6488064 | tf_op jit(solution)/shard_map/reduce_sum | solution.py:58
  272.4 1.0 fusion.18
  (9 shorter events, 0.0 us)
Async XLA Ops:
  7.2 6.0 %copy-start = (bf16[256,1792]{1,0:T(8,128)(2,1)S(1)}, bf16[256,1792]{1,0:T(8,128)(2,1)}, u32[]{:S(2)}) copy-start(bf16[256,1792]{1,0:T(8,128)(2,1)} %param.12) | copy-start | bytes 2752516
  7.2 66.8 %all-gather.2.cloned.1.call-start = ((), (), s32[]{:S(2)}) async-start(), calls=%async_computation.1 | async-start | bytes 4718592 | tf_op jit(solution)/shard_map/all_gather | solution.py:19
  14.4 4.4 %copy-start.4 = (s32[64,3]{0,1:T(4,128)S(1)}, s32[64,3]{0,1:T(4,128)}, u32[]{:S(2)}) copy-start(s32[64,3]{0,1:T(4,128)} %param.13) | copy-start | bytes 2308
  20.2 3.1 %copy-start.5 = (s32[64]{0:T(128)S(1)}, s32[64]{0:T(128)}, u32[]{:S(2)}) copy-start(s32[64]{0:T(128)} %param.14) | copy-start | bytes 772
  119.4 149.1 %all-to-all-start = ((bf16[192,128,128]{2,1,0:T(8,128)(2,1)}), bf16[192,128,128]{2,1,0:T(8,128)(2,1)}, u32[]{:S(2)}, u32[]{:S(2)}) async-start(bf16[192,128,128]{2,1,0:T(8,128)(2,1)} %convert_element_type.32), calls=%async_computation | async-start | bytes 12582912 | tf_op jit(solution)/shard_map/all_to_all | solution.py:55
  130.0 142.4 %copy-start.1 = (f32[3,128,128]{2,1,0:T(8,128)S(1)}, f32[3,128,128]{2,1,0:T(8,128)}, u32[]{:S(2)}) copy-start(f32[3,128,128]{2,1,0:T(8,128)} %param.17) | copy-start | bytes 589828
  130.0 142.4 %copy-start.2 = (f32[3,128,128]{2,1,0:T(8,128)S(1)}, f32[3,128,128]{2,1,0:T(8,128)}, u32[]{:S(2)}) copy-start(f32[3,128,128]{2,1,0:T(8,128)} %param.15) | copy-start | bytes 589828
  130.0 142.4 %copy-start.3 = (f32[3,128,128]{2,1,0:T(8,128)S(1)}, f32[3,128,128]{2,1,0:T(8,128)}, u32[]{:S(2)}) copy-start(f32[3,128,128]{2,1,0:T(8,128)} %param.16) | copy-start | bytes 589828
Sparse Core Ops, SparseCore 0:
  10.1 63.7 all-gather.1
where the time goes:
time: 283 us; the launch traced here: 280 us
  waiting for transfers between devices  188 us (66%)
  local copies, waits for them, and re-layouts  41.9 us (15%)
  other arithmetic  19 us (7%)
  between operations  14.2 us (5%)
  starting transfers between devices  10.6 us (4%)
  matrix products  7.01 us (2%)
    all_to_all x1, waiting for transfers between devices, local(): lax.all_to_all(outgoing.astype(jnp.bfloat16), 'dp', split_axis=0, concat_...  138 us
    all_gather x1, waiting for transfers between devices, local(): gathered = lax.all_gather(features, 'tensor', axis=1, tiled=True)  49.8 us
    scatter x1, local copies, waits for them, and re-layouts, local(): outgoing = jnp.zeros((replicas * capacity, block_size, block_size), jnp.f...  12.1 us
    all_to_all x1, starting transfers between devices, local(): lax.all_to_all(outgoing.astype(jnp.bfloat16), 'dp', split_axis=0, concat_...  10.5 us
    convert_element_type x1, other arithmetic, local(): outgoing.astype(jnp.bfloat16)  8.76 us
    unnamed x16, local copies, waits for them, and re-layouts  7.2 us
    dot_general x1, matrix products, local(): jnp.einsum('tbi,tbj->bij', chosen_rows, chosen_cols, preferred_element_ty...  7.01 us
    reshape x1, local copies, waits for them, and re-layouts, local(): row_cells = gathered.reshape(tokens, -1, block_size)  6.35 us
  transfers between devices with their start and end apart: 2, of which 2 were waited for; matrix products, arithmetic and copies ran while one was open for 5% of the time, Pallas kernels for 0%

commit v1 on v0

v1 whole, which is shorter than its diff:
```python
import functools

import jax
import jax.numpy as jnp
from jax import lax
from jax.experimental import pallas as pl
from jax.experimental.pallas import tpu as pltpu
from jax.sharding import PartitionSpec as P

beta_first = 0.9
beta_second = 0.999
learn_rate = 0.01
epsilon = 1e-08
bias_first = 1.0 - 0.9**10
bias_second = 1.0 - 0.999**10

NX, NY, NZ = 4, 8, 8
BS = 128
COLS = 14
CELLS = 8
LISTED = 64
CAP = 3
MESH = pl.DeviceIdType.MESH
RING = (
    ((0, 0), (0, 1), (1, 0), (1, 1), (2, 0), (2, 1), (3, 0)),
    ((0, 1), (0, 0), (1, 1), (1, 0), (2, 1), (2, 0), (3, 1)),
)
F32, BF16 = jnp.float32, jnp.bfloat16


def kernel(
    feat, gate, up, ghid, blk, own_s, own_v,
    bg_out, cnt_out,
    feats, gate_v, up_v, ghid_v, acts, table_v, table,
    send_c, recv_c, tot,
    x_two, x_in, x_one, x_fwd, x_left, x_right, part,
    y_half, y_half_in, y_out, y_in, gath,
    feat_sem, in_sem, table_sem, zs, zr, cs, cr, xs, xr, ys, yr, gs, gr,
):
    z = lax.axis_index("tensor")
    dp = lax.axis_index("dp")
    core = lax.rem(dp, 2)
    x = lax.rem(dp // 2, NX)
    y = dp // (2 * NX)

    def at(yy, xx, cc):
        return {"dp": (yy * NX + xx) * 2 + cc}

    def shift(v, by, n):
        return lax.rem(v + (by % n), n)

    zdev = ({"tensor": shift(z, 1, NZ)}, {"tensor": shift(z, -1, NZ)})
    xdev = {k: at(y, shift(x, k, NX), core) for k in (1, -1, 2)}
    ydev = (at(shift(y, 1, NY), x, core), at(shift(y, -1, NY), x, core))
    sib = at(y, x, 1 - core)

    in_copies = [
        pltpu.make_async_copy(s, d, in_sem.at[i])
        for i, (s, d) in enumerate(((gate, gate_v), (up, up_v), (ghid, ghid_v)))
    ]
    own_cells = [
        pltpu.make_async_copy(
            feat.at[:, pl.ds(BS * j, BS)], feats.at[z * CELLS + j], feat_sem.at[j]
        )
        for j in range(CELLS)
    ]
    for c in own_cells:
        c.start()
    for c in in_copies:
        c.start()

    barrier = pltpu.get_barrier_semaphore()
    partners = (*zdev, xdev[1], xdev[-1], xdev[2], *ydev, sib)
    for dev in partners:
        pl.semaphore_signal(barrier, inc=1, device_id=dev, device_id_type=MESH)
    pl.semaphore_wait(barrier, len(partners))

    def rcopy(src, dst, ssem, rsem, dev):
        return pltpu.make_async_remote_copy(
            src_ref=src, dst_ref=dst, send_sem=ssem, recv_sem=rsem,
            device_id=dev, device_id_type=MESH,
        )

    def ring(way, k, hop):
        dist, half = RING[way][k]
        src = shift(z, -(dist + hop) if way == 0 else dist + hop, NZ)
        cells = feats.at[pl.ds(src * CELLS + half * 4, 4)]
        return rcopy(cells, cells, zs.at[way, k], zr.at[way, k], zdev[way])

    for c in own_cells:
        c.wait()
    for k in (0, 1):
        for way in (0, 1):
            ring(way, k, 0).start()

    owner_row = own_v[...] // (2 * NX)
    wide = jnp.broadcast_to(owner_row, (LISTED, LISTED))
    tall = wide.T
    lane = lax.broadcasted_iota(jnp.int32, (LISTED, LISTED), 1)
    sub = lax.broadcasted_iota(jnp.int32, (LISTED, LISTED), 0)
    rank_row = jnp.sum(
        ((tall < wide) | ((tall == wide) & (sub < lane))).astype(jnp.int32), axis=0, keepdims=True
    )
    rank_col = jnp.broadcast_to(rank_row, (LISTED, LISTED)).T
    order_row = jnp.sum(jnp.where(rank_col == lane, sub, 0), axis=0, keepdims=True)
    start_row = jnp.sum((tall < lane).astype(jnp.int32), axis=0, keepdims=True)
    table_v[...] = jnp.zeros_like(table_v)
    table_v[0:1, 0:LISTED] = order_row
    table_v[1:2, 0:LISTED] = rank_row
    table_v[2:3, 0:LISTED] = start_row
    to_smem = pltpu.make_async_copy(table_v, table, table_sem)
    to_smem.start()

    for c in in_copies:
        c.wait()

    def make_acts(c, carry):
        cols = pl.ds(pl.multiple_of(c * BS, BS), BS)
        g = gate_v[:, cols].astype(F32)
        h = ghid_v[:, cols].astype(F32)
        u = up_v[:, cols].astype(F32)
        s = jax.nn.sigmoid(g)
        d_up = (h * (g * s)).astype(BF16)
        d_gate = (h * u * (s * (1.0 + g * (1.0 - s)))).astype(BF16)
        acts[c] = d_gate.T
        acts[c + COLS] = d_up.T
        return carry

    for k in range(2, 7):
        lax.fori_loop(3 * (k - 2), min(3 * (k - 1), COLS), make_acts, 0)
        for way in (0, 1):
            ring(way, k - 2, 1).wait_recv()
            ring(way, k, 0).start()
    to_smem.wait()

    def find(k, carry):
        count, q0, q1, q2 = carry
        mine = own_s[k] == dp
        q = table[1, k]
        q0 = jnp.where(mine & (count == 0), q, q0)
        q1 = jnp.where(mine & (count == 1), q, q1)
        q2 = jnp.where(mine & (count == 2), q, q2)
        return count + mine.astype(jnp.int32), q0, q1, q2

    zero = jnp.int32(0)
    count, *mine_at = lax.fori_loop(0, LISTED, find, (zero, zero, zero, zero))
    cnt_out[0] = count

    for k in (5, 6):
        for way in (0, 1):
            ring(way, k, 1).wait_recv()
    for k in range(7):
        for way in (0, 1):
            ring(way, k, 0).wait_send()

    def product(xx, cc, i):
        k = table[0, i * 8 + xx * 2 + cc]
        a = acts[blk[0, k] * COLS + blk[2, k]]
        return jnp.dot(a, feats[blk[1, k]], preferred_element_type=F32)

    def products(dst, n, xx, cc):
        def some(i4, carry):
            for i in range(4):
                dst[n, i4 * 4 + i] = product(xx, cc, i4 * 4 + i)
            return carry

        lax.fori_loop(0, 2, some, 0)

    rel = (2, 1, 3, 0)
    to_sib = []
    for n in range(4):
        products(send_c, n, shift(x, rel[n], NX), 1 - core)
        c = rcopy(send_c.at[n], recv_c.at[n], cs.at[n], cr.at[n], sib)
        c.start()
        to_sib.append(c)

    lo, hi = pl.ds(0, 4), pl.ds(4, 4)
    two_plus = rcopy(x_two.at[lo], x_in.at[0], xs.at[0], xr.at[0], xdev[1])
    two_minus = rcopy(x_two.at[hi], x_in.at[1], xs.at[1], xr.at[1], xdev[-1])
    one_plus = rcopy(x_one.at[0], x_left.at[hi], xs.at[2], xr.at[2], xdev[1])
    one_minus = rcopy(x_one.at[1], x_right.at[lo], xs.at[3], xr.at[3], xdev[-1])
    fwd_plus = rcopy(x_fwd.at[0], x_left.at[lo], xs.at[4], xr.at[4], xdev[1])
    fwd_minus = rcopy(x_fwd.at[1], x_right.at[hi], xs.at[5], xr.at[5], xdev[-1])
    for n in range(4):
        products(tot, n, shift(x, rel[n], NX), core)
        to_sib[n].wait_recv()
        tot[n] = tot[n] + recv_c[n]
        if n == 0:
            x_two[...] = tot[0].astype(BF16)
            two_plus.start()
            two_minus.start()
        if n == 1:
            x_one[0] = tot[1, 4:8].astype(BF16)
            one_plus.start()
        if n == 2:
            x_one[1] = tot[2, 0:4].astype(BF16)
            one_minus.start()
    two_plus.wait_recv()
    x_fwd[0] = (tot[1, 0:4] + x_in[0].astype(F32)).astype(BF16)
    fwd_plus.start()
    two_minus.wait_recv()
    x_fwd[1] = (tot[2, 4:8] + x_in[1].astype(F32)).astype(BF16)
    fwd_minus.start()
    for c in (one_plus, one_minus, fwd_plus, fwd_minus):
        c.wait_recv()
    part[...] = tot[3] + x_left[...].astype(F32) + x_right[...].astype(F32)

    col = x * 2 + core

    def first_of(yy, column):
        return (table[2, yy] + (7 - column)) // 8

    def term(yy, e):
        return part[jnp.minimum(first_of(yy, col) + e, 7)]

    rows = (slice(0, 64), slice(64, 128))
    half_copy = [
        rcopy(y_half.at[w], y_half_in.at[w], ys.at[w, 0], yr.at[w, 0], ydev[w]) for w in (0, 1)
    ]
    y_copy = [
        [
            rcopy(y_out.at[w, t], y_in.at[w, t], ys.at[w, t + 1], yr.at[w, t + 1], ydev[w])
            for t in range(3)
        ]
        for w in (0, 1)
    ]
    for w in (0, 1):
        for e in range(CAP):
            y_half[w, e] = term(shift(y, 4, NY), e)[rows[w]].astype(BF16)
        half_copy[w].start()
    for t in range(3):
        for w in (0, 1):
            yy = shift(y, 3 - t if w == 0 else t - 3, NY)
            if t == 0:
                half_copy[w].wait_recv()
            else:
                y_copy[w][t - 1].wait_recv()
            for e in range(CAP):
                v = term(yy, e)
                if t == 0:
                    got = y_half_in[w, e].astype(F32)
                    y_out[w, t, e, rows[w]] = (v[rows[w]] + got).astype(BF16)
                    y_out[w, t, e, rows[1 - w]] = v[rows[1 - w]].astype(BF16)
                else:
                    y_out[w, t, e] = (v + y_in[w, t - 1, e].astype(F32)).astype(BF16)
            y_copy[w][t].start()
    for w in (0, 1):
        y_copy[w][2].wait_recv()
    for e in range(CAP):
        gath[col * CAP + e] = (
            term(y, e) + y_in[0, 2, e].astype(F32) + y_in[1, 2, e].astype(F32)
        )

    def column(cc):
        return gath.at[pl.ds(cc * CAP, CAP)]

    x_copy = []
    for n, k in enumerate((2, 1, -1)):
        c = rcopy(column(col), column(col), gs.at[n], gr.at[n], xdev[k])
        c.start()
        x_copy.append(c)
    sib_copy = [rcopy(column(col), column(col), gs.at[3], gr.at[3], sib)]
    sib_copy[0].start()
    for n, k in ((1, 1), (2, -1), (0, 2)):
        x_copy[n].wait_recv()
        came = column(shift(x, -k, NX) * 2 + core)
        c = rcopy(came, came, gs.at[4 + n], gr.at[4 + n], sib)
        c.start()
        sib_copy.append(c)
    for c in sib_copy:
        c.wait_recv()
    for s in range(CAP):
        q = mine_at[s]
        column_of = lax.rem(q, 8)
        e = q // 8 - first_of(y, column_of)
        at_row = jnp.clip(column_of * CAP + e, 0, 8 * CAP - 1)
        bg_out[s] = gath[at_row].T

    for c in (*to_sib, two_plus, two_minus, one_plus, one_minus, fwd_plus, fwd_minus,
              *half_copy, *y_copy[0], *y_copy[1], *x_copy, *sib_copy):
        c.wait_send()


def local(features, gate_pre, up_pre, grad_hidden, blocks, owner, weights, moment1, moment2):
    any_ = pl.BlockSpec(memory_space=pl.ANY)
    smem = pl.BlockSpec(memory_space=pltpu.SMEM)
    vmem = pl.BlockSpec(memory_space=pltpu.VMEM)
    tokens = features.shape[0]
    dma = pltpu.SemaphoreType.DMA
    block_grad, count = pl.pallas_call(
        kernel,
        out_shape=(
            jax.ShapeDtypeStruct((CAP, BS, BS), F32),
            jax.ShapeDtypeStruct((1,), jnp.int32),
        ),
        in_specs=[any_, any_, any_, any_, smem, smem, vmem],
        out_specs=(vmem, smem),
        scratch_shapes=[
            pltpu.VMEM((NZ * CELLS, tokens, BS), BF16),
            pltpu.VMEM(gate_pre.shape, BF16),
            pltpu.VMEM(gate_pre.shape, BF16),
            pltpu.VMEM(gate_pre.shape, BF16),
            pltpu.VMEM((2 * COLS, BS, tokens), BF16),
            pltpu.VMEM((8, 128), jnp.int32),
            pltpu.SMEM((8, 128), jnp.int32),
            pltpu.VMEM((4, 8, BS, BS), F32),
            pltpu.VMEM((4, 8, BS, BS), F32),
            pltpu.VMEM((4, 8, BS, BS), F32),
            pltpu.VMEM((8, BS, BS), BF16),
            pltpu.VMEM((2, 4, BS, BS), BF16),
            pltpu.VMEM((2, 4, BS, BS), BF16),
            pltpu.VMEM((2, 4, BS, BS), BF16),
            pltpu.VMEM((8, BS, BS), BF16),
            pltpu.VMEM((8, BS, BS), BF16),
            pltpu.VMEM((8, BS, BS), F32),
            pltpu.VMEM((2, CAP, BS // 2, BS), BF16),
            pltpu.VMEM((2, CAP, BS // 2, BS), BF16),
            pltpu.VMEM((2, 3, CAP, BS, BS), BF16),
            pltpu.VMEM((2, 3, CAP, BS, BS), BF16),
            pltpu.VMEM((8 * CAP, BS, BS), F32),
            dma((CELLS,)),
            dma((3,)),
            dma,
            dma((2, 7)),
            dma((2, 7)),
            dma((4,)),
            dma((4,)),
            dma((6,)),
            dma((6,)),
            dma((2, 4)),
            dma((2, 4)),
            dma((7,)),
            dma((7,)),
        ],
        compiler_params=pltpu.CompilerParams(
            collective_id=0, has_side_effects=True, vmem_limit_bytes=48 * 2**20
        ),
        cost_estimate=pl.CostEstimate(
            flops=2 * LISTED * tokens * BS * BS, bytes_accessed=4 * 2**20, transcendentals=tokens * COLS * BS
        ),
        name="block_grads",
    )(features, gate_pre, up_pre, grad_hidden, blocks.T, owner, owner.reshape(1, LISTED))
    is_valid = (jnp.arange(CAP, dtype=jnp.int32) < count[0])[:, None, None]
    first_new = beta_first * moment1 + (1.0 - beta_first) * block_grad
    second_new = beta_second * moment2 + (1.0 - beta_second) * block_grad * block_grad
    weight_new = weights - learn_rate * (first_new / bias_first) / (
        jnp.sqrt(second_new / bias_second) + epsilon
    )
    return (
        jnp.where(is_valid, weight_new, weights),
        jnp.where(is_valid, first_new, moment1),
        jnp.where(is_valid, second_new, moment2),
    )


def solution(mesh):
    tokens = P("dp", "tensor")
    state = P(("dp", "tensor"), None, None)
    return jax.shard_map(
        local,
        mesh=mesh,
        in_specs=(tokens,) * 4 + (P("tensor", None), P("tensor")) + (state,) * 3,
        out_specs=(state,) * 3,
        check_vma=False,
    )
```

time: 283 us -> 105 us (0.37)
  waiting for transfers between devices: 188 us -> 0 us
  Pallas kernels: 0 us -> 97.2 us
  local copies, waits for them, and re-layouts: 41.9 us -> 5.26 us
  other arithmetic: 19 us -> 1.64 us
  between operations: 14.2 us -> 0.69 us
  starting transfers between devices: 10.6 us -> 0 us
  matrix products: 7.01 us -> 0 us
    all_to_all x1 -> x0, waiting for transfers between devices: 138 us -> none  [local(): lax.all_to_all(outgoing.astype(jnp.bfloat16), 'dp', split_axis=0, concat_...]
    pallas_call x0 -> x1, Pallas kernels: none -> 97.2 us  [local(): pl.pallas_call(kernel, out_shape=(jax.ShapeDtypeStruct((CAP, BS, BS), F32...]
    all_gather x1 -> x0, waiting for transfers between devices: 49.8 us -> none  [local(): gathered = lax.all_gather(features, 'tensor', axis=1, tiled=True)]
    scatter x1 -> x0, local copies, waits for them, and re-layouts: 12.1 us -> none  [local(): outgoing = jnp.zeros((replicas * capacity, block_size, block_size), jnp.f...]
    convert_element_type x2 -> x0, other arithmetic: 11.2 us -> none  [the longest x1 8.76 us: local(): outgoing.astype(jnp.bfloat16)]
    all_to_all x1 -> x0, starting transfers between devices: 10.5 us -> none  [local(): lax.all_to_all(outgoing.astype(jnp.bfloat16), 'dp', split_axis=0, concat_...]
    reshape x3 -> x0, local copies, waits for them, and re-layouts: 8.26 us -> none  [the longest x1 6.35 us: local(): row_cells = gathered.reshape(tokens, -1, block_size)]
    gather x2 -> x0, local copies, waits for them, and re-layouts: 8.26 us -> none  [the longest x1 5.21 us: local(): chosen_rows = jnp.take(row_cells, blocks[:, 1], axis=1)]
  transfers between devices with their start and end apart: 2 -> 0, of which waited for: 2 -> 0; matrix products, arithmetic and copies ran while one was open for 5% -> 0% of each run, Pallas kernels for 0% -> 0%
where the time goes in v1:
time: 105 us
  Pallas kernels  97.2 us (93%)
  local copies, waits for them, and re-layouts  5.26 us (5%)
  other arithmetic  1.64 us (2%)
    pallas_call x1, Pallas kernels, local(): pl.pallas_call(kernel, out_shape=(jax.ShapeDtypeStruct((CAP, BS, BS), F32...  97.2 us
    unnamed x18, local copies, waits for them, and re-layouts  5.26 us

profile of v1, /device:TPU:1, one launch (start us, length us, event | category | flops | bytes accessed | tf_op | source)
XLA Modules:
  0.0 104.8 jit_solution(6535261248827545108)
XLA Ops:
  0.6 0.0 copy-start.4
  0.6 0.0 copy-start.5
  0.7 0.7 copy-done.4
  1.3 0.0 copy-done.5
  1.3 0.0 copy-start
  1.3 1.2 %copy-done = bf16[256,1792]{1,0:T(8,128)(2,1)S(1)} copy-done((bf16[256,1792]{1,0:T(8,128)(2,1)S(1)}, bf16[256,1792]{1,0:T(8,128)(2,1)}, u32[]{:S(2)}) %copy-start) | copy-done | bytes 917528
  2.5 0.0 copy-start.1
  2.5 1.2 %copy-done.1 = bf16[256,1792]{1,0:T(8,128)(2,1)S(1)} copy-done((bf16[256,1792]{1,0:T(8,128)(2,1)S(1)}, bf16[256,1792]{1,0:T(8,128)(2,1)}, u32[]{:S(2)}) %copy-start.1) | copy-done | bytes 917528
  3.7 0.0 copy-start.2
  3.7 1.2 %copy-done.2 = bf16[256,1792]{1,0:T(8,128)(2,1)S(1)} copy-done((bf16[256,1792]{1,0:T(8,128)(2,1)S(1)}, bf16[256,1792]{1,0:T(8,128)(2,1)}, u32[]{:S(2)}) %copy-start.2) | copy-done | bytes 917528
  4.9 0.0 copy-start.3
  4.9 1.0 copy-done.3
  5.9 0.0 copy-start.6
  5.9 0.0 copy-start.7
  5.9 0.0 copy-start.8
  5.9 97.2 %block_grads.1 = (f32[3,128,128]{2,1,0:T(8,128)S(1)}, s32[1]{0:T(128)}) custom-call(bf16[256,1024]{1,0:T(8,128)(2,1)S(1)} %copy-done.3, bf16[256,1792]{1,0:T(8,128)(2,1)S(1)} %copy-done, bf16[256,1792]{1,0:T(8,128)(2,1)S(1)} %copy-done.1, bf16[256,1792]{1,0:T(8,128)(2,1)S(1)} %copy-done.2, s32[3,64]{1,0:T(4,128)S(1)} %bitcast.3, s32[64]{0:T(128)S(1)} %copy-done.5, ...), custom_call_target="tpu_custom_call" | custom-call | flops 536870912 | bytes 4194304 | tf_op jit(solution)/shard_map/block_grads/pallas_call | solution.py:290
  103.2 0.6 iota_compare_fusion
  103.8 0.0 copy-done.6
  103.8 0.0 copy-done.7
  103.8 0.0 copy-done.8
  103.8 1.0 fusion.2
Async XLA Ops:
  0.6 0.7 copy-start.4
  0.6 0.7 copy-start.5
  1.3 1.2 %copy-start = (bf16[256,1792]{1,0:T(8,128)(2,1)S(1)}, bf16[256,1792]{1,0:T(8,128)(2,1)}, u32[]{:S(2)}) copy-start(bf16[256,1792]{1,0:T(8,128)(2,1)} %gate.1) | copy-start | bytes 2752516
  2.5 1.2 %copy-start.1 = (bf16[256,1792]{1,0:T(8,128)(2,1)S(1)}, bf16[256,1792]{1,0:T(8,128)(2,1)}, u32[]{:S(2)}) copy-start(bf16[256,1792]{1,0:T(8,128)(2,1)} %up.1) | copy-start | bytes 2752516
  3.7 1.2 %copy-start.2 = (bf16[256,1792]{1,0:T(8,128)(2,1)S(1)}, bf16[256,1792]{1,0:T(8,128)(2,1)}, u32[]{:S(2)}) copy-start(bf16[256,1792]{1,0:T(8,128)(2,1)} %ghid.1) | copy-start | bytes 2752516
  4.9 1.0 copy-start.3
  5.9 97.9 %copy-start.6 = (f32[3,128,128]{2,1,0:T(8,128)S(1)}, f32[3,128,128]{2,1,0:T(8,128)}, u32[]{:S(2)}) copy-start(f32[3,128,128]{2,1,0:T(8,128)} %param.17) | copy-start | bytes 589828
  5.9 97.9 %copy-start.7 = (f32[3,128,128]{2,1,0:T(8,128)S(1)}, f32[3,128,128]{2,1,0:T(8,128)}, u32[]{:S(2)}) copy-start(f32[3,128,128]{2,1,0:T(8,128)} %param.15) | copy-start | bytes 589828
  5.9 97.9 %copy-start.8 = (f32[3,128,128]{2,1,0:T(8,128)S(1)}, f32[3,128,128]{2,1,0:T(8,128)}, u32[]{:S(2)}) copy-start(f32[3,128,128]{2,1,0:T(8,128)} %param.16) | copy-start | bytes 589828

commit v2 on v1

v2 whole, which is shorter than its diff:
```python
import functools

import jax
import jax.numpy as jnp
from jax import lax
from jax.experimental import pallas as pl
from jax.experimental.pallas import tpu as pltpu
from jax.sharding import PartitionSpec as P

beta_first = 0.9
beta_second = 0.999
learn_rate = 0.01
epsilon = 1e-08
bias_first = 1.0 - 0.9**10
bias_second = 1.0 - 0.999**10

NX, NY, NZ = 4, 8, 8
BS = 128
COLS = 14
CELLS = 8
LISTED = 64
CAP = 3
MESH = pl.DeviceIdType.MESH
PARTS = 4
ROWS = BS // PARTS
LAG = 0
CHUNK = 4
PER = CELLS // CHUNK
RING = tuple(
    [(d, c) for d in range(3) for c in order] + [(3, c) for c in order[: PER // 2]]
    for order in (list(range(PER)), list(range(PER))[::-1])
)
HOPS = len(RING[0])
F32, BF16 = jnp.float32, jnp.bfloat16


def kernel(
    feat, gate, up, ghid, blk, own_s, own_v,
    bg_out, cnt_out,
    feats, gate_v, up_v, ghid_v, acts, table_v, table,
    send_c, recv_c, tot,
    x_two, x_in, x_one, x_fwd, x_left, x_right, part,
    y_out, y_in, gath,
    feat_sem, in_sem, table_sem, zs, zr, cs, cr, xs, xr, ys, yr, gs, gr,
):
    z = lax.axis_index("tensor")
    dp = lax.axis_index("dp")
    core = lax.rem(dp, 2)
    x = lax.rem(dp // 2, NX)
    y = dp // (2 * NX)

    def at(yy, xx, cc):
        return {"dp": (yy * NX + xx) * 2 + cc}

    def shift(v, by, n):
        return lax.rem(v + (by % n), n)

    zdev = ({"tensor": shift(z, 1, NZ)}, {"tensor": shift(z, -1, NZ)})
    xdev = {k: at(y, shift(x, k, NX), core) for k in (1, -1, 2)}
    ydev = {k: at(shift(y, k, NY), x, core) for k in (1, -1, 2, -2)}
    sib = at(y, x, 1 - core)

    in_copies = [
        pltpu.make_async_copy(s, d, in_sem.at[i])
        for i, (s, d) in enumerate(((gate, gate_v), (up, up_v), (ghid, ghid_v)))
    ]
    own_cells = [
        pltpu.make_async_copy(
            feat.at[:, pl.ds(BS * j, BS)], feats.at[z * CELLS + j], feat_sem.at[j]
        )
        for j in range(CELLS)
    ]
    for c in own_cells:
        c.start()
    for c in in_copies:
        c.start()

    barrier = pltpu.get_barrier_semaphore()
    partners = (*zdev, *xdev.values(), *ydev.values(), sib)
    for dev in partners:
        pl.semaphore_signal(barrier, inc=1, device_id=dev, device_id_type=MESH)
    pl.semaphore_wait(barrier, len(partners))

    def rcopy(src, dst, ssem, rsem, dev):
        return pltpu.make_async_remote_copy(
            src_ref=src, dst_ref=dst, send_sem=ssem, recv_sem=rsem,
            device_id=dev, device_id_type=MESH,
        )

    def ring(way, k, hop):
        dist, half = RING[way][k]
        src = shift(z, -(dist + hop) if way == 0 else dist + hop, NZ)
        cells = feats.at[pl.ds(src * CELLS + half * CHUNK, CHUNK)]
        return rcopy(cells, cells, zs.at[way, k], zr.at[way, k], zdev[way])

    for c in own_cells:
        c.wait()
    for k in range(PER):
        for way in (0, 1):
            ring(way, k, 0).start()

    owner_row = own_v[...] // (2 * NX)
    wide = jnp.broadcast_to(owner_row, (LISTED, LISTED))
    tall = wide.T
    lane = lax.broadcasted_iota(jnp.int32, (LISTED, LISTED), 1)
    sub = lax.broadcasted_iota(jnp.int32, (LISTED, LISTED), 0)
    rank_row = jnp.sum(
        ((tall < wide) | ((tall == wide) & (sub < lane))).astype(jnp.int32), axis=0, keepdims=True
    )
    rank_col = jnp.broadcast_to(rank_row, (LISTED, LISTED)).T
    order_row = jnp.sum(jnp.where(rank_col == lane, sub, 0), axis=0, keepdims=True)
    start_row = jnp.sum((tall < lane).astype(jnp.int32), axis=0, keepdims=True)
    table_v[...] = jnp.zeros_like(table_v)
    table_v[0:1, 0:LISTED] = order_row
    table_v[1:2, 0:LISTED] = rank_row
    table_v[2:3, 0:LISTED] = start_row
    to_smem = pltpu.make_async_copy(table_v, table, table_sem)
    to_smem.start()

    for c in in_copies:
        c.wait()

    def make_acts(c, carry):
        cols = pl.ds(pl.multiple_of(c * BS, BS), BS)
        g = gate_v[:, cols].astype(F32)
        h = ghid_v[:, cols].astype(F32)
        u = up_v[:, cols].astype(F32)
        s = jax.nn.sigmoid(g)
        d_up = (h * (g * s)).astype(BF16)
        d_gate = (h * u * (s * (1.0 + g * (1.0 - s)))).astype(BF16)
        acts[c] = d_gate.T
        acts[c + COLS] = d_up.T
        return carry

    done = 0
    for k in range(PER, HOPS):
        upto = min(COLS, (k - PER + 1) * COLS // (HOPS - PER - 1))
        if upto > done:
            lax.fori_loop(done, upto, make_acts, 0)
            done = upto
        for way in (0, 1):
            ring(way, k - PER, 1).wait_recv()
            ring(way, k, 0).start()
    to_smem.wait()

    def find(k, carry):
        count, q0, q1, q2 = carry
        mine = own_s[k] == dp
        q = table[1, k]
        q0 = jnp.where(mine & (count == 0), q, q0)
        q1 = jnp.where(mine & (count == 1), q, q1)
        q2 = jnp.where(mine & (count == 2), q, q2)
        return count + mine.astype(jnp.int32), q0, q1, q2

    zero = jnp.int32(0)
    count, *mine_at = lax.fori_loop(0, LISTED, find, (zero, zero, zero, zero))
    cnt_out[0] = count

    for k in range(HOPS - PER, HOPS):
        for way in (0, 1):
            ring(way, k, 1).wait_recv()
    for k in range(HOPS):
        for way in (0, 1):
            ring(way, k, 0).wait_send()

    def product(xx, cc, i):
        k = table[0, i * 8 + xx * 2 + cc]
        a = acts[blk[0, k] * COLS + blk[2, k]]
        return jnp.dot(a, feats[blk[1, k]], preferred_element_type=F32)

    def products(dst, n, xx, cc):
        for i in range(8):
            dst[n, i] = product(xx, cc, i)

    rel = (2, 1, 3, 0)
    sent = []

    def send(*copy):
        c = rcopy(*copy)
        c.start()
        sent.append(c)
        return c

    to_sib = {}

    def for_sib(n):
        products(send_c, n, shift(x, rel[n], NX), 1 - core)
        to_sib[n] = send(send_c.at[n], recv_c.at[n], cs.at[n], cr.at[n], sib)

    def for_me(n):
        products(tot, n, shift(x, rel[n], NX), core)

    def rows_of(h):
        return pl.ds(h * ROWS, ROWS)

    lo, hi = pl.ds(0, 4), pl.ds(4, 4)
    along_x = [{} for _ in range(PARTS)]

    def to_x(h, name, n, src, dst, step):
        along_x[h][name] = send(src, dst, xs.at[h, n], xr.at[h, n], xdev[step])

    def core_sum(n):
        to_sib[n].wait_recv()
        tot[n] = tot[n] + recv_c[n]
        for h in range(PARTS if n == 0 else 0):
            if n == 0:
                x_two[h] = tot[0, :, rows_of(h)].astype(BF16)
                to_x(h, "two+", 0, x_two.at[h, lo], x_in.at[h, 0], 1)
                to_x(h, "two-", 1, x_two.at[h, hi], x_in.at[h, 1], -1)

    for_sib(0)
    for_sib(1)
    for_me(0)
    core_sum(0)
    for_me(1)
    for_sib(2)
    core_sum(1)
    for_me(2)
    for_sib(3)
    core_sum(2)
    for_me(3)
    core_sum(3)

    col = x * 2 + core

    def first_of(yy, column):
        return (table[2, yy] + (7 - column)) // 8

    def column(cc, h):
        return gath.at[pl.ds(cc * CAP, CAP), rows_of(h)]

    def tail(h):
        mine = rows_of(h)
        moves = along_x[h]
        x_one[h, 0] = tot[1, hi, mine].astype(BF16)
        to_x(h, "one+", 2, x_one.at[h, 0], x_left.at[h, hi], 1)
        x_one[h, 1] = tot[2, lo, mine].astype(BF16)
        to_x(h, "one-", 3, x_one.at[h, 1], x_right.at[h, lo], -1)
        moves["two+"].wait_recv()
        x_fwd[h, 0] = (tot[1, lo, mine] + x_in[h, 0].astype(F32)).astype(BF16)
        to_x(h, "fwd+", 4, x_fwd.at[h, 0], x_left.at[h, lo], 1)
        moves["two-"].wait_recv()
        x_fwd[h, 1] = (tot[2, hi, mine] + x_in[h, 1].astype(F32)).astype(BF16)
        to_x(h, "fwd-", 5, x_fwd.at[h, 1], x_right.at[h, hi], -1)
        yield
        for name in ("one+", "one-", "fwd+", "fwd-"):
            moves[name].wait_recv()
        part[:, mine] = tot[3, :, mine] + x_left[h].astype(F32) + x_right[h].astype(F32)

        def term(yy, e):
            return part[jnp.minimum(first_of(yy, col) + e, 7), mine]

        def along_y(way, kind, dist, hop, came=()):
            sign = 1 if way == 0 else -1
            yy = shift(y, sign * dist, NY)
            for e in range(CAP):
                v = term(yy, e)
                for k in came:
                    v = v + y_in[h, way, k, e].astype(F32)
                y_out[h, way, kind, e] = v.astype(BF16)
            return send(
                y_out.at[h, way, kind], y_in.at[h, way, kind],
                ys.at[h, way, kind], yr.at[h, way, kind], ydev[sign * hop],
            )

        far = h % 2
        ways = (far, 1 - far)
        third = {w: along_y(w, 0, 3, 1) for w in ways}
        fourth = along_y(far, 2, 4, 2)
        first = {w: along_y(w, 1, 1, 1) for w in ways}
        yield
        second = {}
        for w in ways:
            third[w].wait_recv()
            if w == far:
                fourth.wait_recv()
            second[w] = along_y(w, 3, 2, 2, (0, 2) if w == far else (0,))
        yield
        for w in ways:
            first[w].wait_recv()
            second[w].wait_recv()
        for e in range(CAP):
            v = term(y, e)
            for w in (0, 1):
                v = v + (y_in[h, w, 1, e].astype(F32) + y_in[h, w, 3, e].astype(F32))
            gath[col * CAP + e, mine] = v

        own = column(col, h)
        x_copy = [send(own, own, gs.at[h, n], gr.at[h, n], xdev[k]) for n, k in enumerate((2, 1, -1))]
        sib_copy = [send(own, own, gs.at[h, 3], gr.at[h, 3], sib)]
        yield
        for n, k in ((1, 1), (2, -1), (0, 2)):
            x_copy[n].wait_recv()
            came = column(shift(x, -k, NX) * 2 + core, h)
            sib_copy.append(send(came, came, gs.at[h, 4 + n], gr.at[h, 4 + n], sib))
        yield
        for c in sib_copy:
            c.wait_recv()

    turns = [tail(h) for h in range(PARTS)]
    for turn in turns:
        next(turn)
    running, slot = set(range(PARTS)), 0
    while running:
        for h in sorted(running):
            if h * LAG <= slot and next(turns[h], turns) is turns:
                running.remove(h)
        slot += 1

    for s in range(CAP):
        q = mine_at[s]
        column_of = lax.rem(q, 8)
        e = q // 8 - first_of(y, column_of)
        at_row = jnp.clip(column_of * CAP + e, 0, 8 * CAP - 1)
        bg_out[s] = gath[at_row].T

    for c in sent:
        c.wait_send()


def local(features, gate_pre, up_pre, grad_hidden, blocks, owner, weights, moment1, moment2):
    hbm = pl.BlockSpec(memory_space=pltpu.HBM)
    smem = pl.BlockSpec(memory_space=pltpu.SMEM)
    vmem = pl.BlockSpec(memory_space=pltpu.VMEM)
    tokens = features.shape[0]
    dma = pltpu.SemaphoreType.DMA
    block_grad, count = pl.pallas_call(
        kernel,
        out_shape=(
            jax.ShapeDtypeStruct((CAP, BS, BS), F32),
            jax.ShapeDtypeStruct((1,), jnp.int32),
        ),
        in_specs=[hbm, hbm, hbm, hbm, smem, smem, vmem],
        out_specs=(vmem, smem),
        scratch_shapes=[
            pltpu.VMEM((NZ * CELLS, tokens, BS), BF16),
            pltpu.VMEM(gate_pre.shape, BF16),
            pltpu.VMEM(gate_pre.shape, BF16),
            pltpu.VMEM(gate_pre.shape, BF16),
            pltpu.VMEM((2 * COLS, BS, tokens), BF16),
            pltpu.VMEM((8, 128), jnp.int32),
            pltpu.SMEM((8, 128), jnp.int32),
            pltpu.VMEM((4, 8, BS, BS), F32),
            pltpu.VMEM((4, 8, BS, BS), F32),
            pltpu.VMEM((4, 8, BS, BS), F32),
            pltpu.VMEM((PARTS, 8, ROWS, BS), BF16),
            pltpu.VMEM((PARTS, 2, 4, ROWS, BS), BF16),
            pltpu.VMEM((PARTS, 2, 4, ROWS, BS), BF16),
            pltpu.VMEM((PARTS, 2, 4, ROWS, BS), BF16),
            pltpu.VMEM((PARTS, 8, ROWS, BS), BF16),
            pltpu.VMEM((PARTS, 8, ROWS, BS), BF16),
            pltpu.VMEM((8, BS, BS), F32),
            pltpu.VMEM((PARTS, 2, 4, CAP, ROWS, BS), BF16),
            pltpu.VMEM((PARTS, 2, 4, CAP, ROWS, BS), BF16),
            pltpu.VMEM((8 * CAP, BS, BS), F32),
            dma((CELLS,)),
            dma((3,)),
            dma,
            dma((2, HOPS)),
            dma((2, HOPS)),
            dma((4,)),
            dma((4,)),
            dma((PARTS, 6)),
            dma((PARTS, 6)),
            dma((PARTS, 2, 4)),
            dma((PARTS, 2, 4)),
            dma((PARTS, 7)),
            dma((PARTS, 7)),
        ],
        compiler_params=pltpu.CompilerParams(
            collective_id=0, has_side_effects=True, vmem_limit_bytes=60 * 2**20
        ),
        cost_estimate=pl.CostEstimate(
            flops=2 * LISTED * tokens * BS * BS, bytes_accessed=4 * 2**20, transcendentals=tokens * COLS * BS
        ),
        name="block_grads",
    )(features, gate_pre, up_pre, grad_hidden, blocks.T, owner, owner.reshape(1, LISTED))
    is_valid = (jnp.arange(CAP, dtype=jnp.int32) < count[0])[:, None, None]
    first_new = beta_first * moment1 + (1.0 - beta_first) * block_grad
    second_new = beta_second * moment2 + (1.0 - beta_second) * block_grad * block_grad
    weight_new = weights - learn_rate * (first_new / bias_first) / (
        jnp.sqrt(second_new / bias_second) + epsilon
    )
    return (
        jnp.where(is_valid, weight_new, weights),
        jnp.where(is_valid, first_new, moment1),
        jnp.where(is_valid, second_new, moment2),
    )


def solution(mesh):
    tokens = P("dp", "tensor")
    state = P(("dp", "tensor"), None, None)
    return jax.shard_map(
        local,
        mesh=mesh,
        in_specs=(tokens,) * 4 + (P("tensor", None), P("tensor")) + (state,) * 3,
        out_specs=(state,) * 3,
        check_vma=False,
    )
```

time: 105 us -> 94.2 us (0.90)
  Pallas kernels: 97.2 us -> 90.8 us
  local copies, waits for them, and re-layouts: 5.26 us -> 0.01 us
    pallas_call x1, Pallas kernels: 97.2 us -> 90.8 us  [local(): pl.pallas_call(kernel, out_shape=(jax.ShapeDtypeStruct((CAP, BS, BS), F32...]
    unnamed x18 -> x6, local copies, waits for them, and re-layouts: 5.26 us -> 0.01 us
where the time goes in v2:
time: 94.2 us; the launch traced here: 94 us
  Pallas kernels  90.8 us (96%)
  other arithmetic  2.56 us (3%)
    pallas_call x1, Pallas kernels, local(): pl.pallas_call(kernel, out_shape=(jax.ShapeDtypeStruct((CAP, BS, BS), F32...  90.8 us
    select_n x1, other arithmetic, local(): jnp.where(is_valid, second_new, moment2)  1.92 us

profile of v2, /device:TPU:1, one launch (start us, length us, event | category | flops | bytes accessed | tf_op | source)
XLA Modules:
  0.0 94.0 jit_solution(6974781715965596558)
XLA Ops:
  0.6 0.0 copy-start
  0.6 0.0 copy-start.1
  0.7 0.0 copy-start.2
  0.7 90.8 %block_grads.1 = (f32[3,128,128]{2,1,0:T(8,128)}, s32[1]{0:T(128)}) custom-call(bf16[256,1024]{1,0:T(8,128)(2,1)} %feat.1, bf16[256,1792]{1,0:T(8,128)(2,1)} %gate.1, bf16[256,1792]{1,0:T(8,128)(2,1)} %up.1, bf16[256,1792]{1,0:T(8,128)(2,1)} %ghid.1, s32[3,64]{1,0:T(4,128)} %bitcast.3, s32[64]{0:T(128)} %own_s.1, s32[1,64]{1,0:T(1,128)} %bitcast.4), custom_call_target="tpu_custom_call" | custom-call | flops 536870912 | bytes 4194304 | tf_op jit(solution)/shard_map/block_grads/pallas_call | solution.py:327
  91.4 0.6 iota_compare_fusion
  92.1 0.0 copy-done
  92.1 0.0 copy-done.1
  92.1 0.0 copy-done.2
  92.1 1.9 %fusion.2 = (f32[3,128,128]{2,1,0:T(8,128)}, f32[3,128,128]{2,1,0:T(8,128)}, f32[3,128,128]{2,1,0:T(8,128)}) fusion(f32[3,128,128]{2,1,0:T(8,128)S(1)} %copy-done, f32[3,128,128]{2,1,0:T(8,128)} %get-tuple-element.6, pred[3]{0:T(512)(128)(4,1)S(1)} %iota_compare_fusion, f32[3,128,128]{2,1,0:T(8,128)S(1)} %copy-done.1, f32[3,128,128]{2,1,0:T(8,128)S(1)} %copy-done.2), kind=kLoop, calls=%fused_computation.5 | loop fusion | flops 737280 | bytes 1376259 | tf_op jit(solution)/shard_map/jit(_where)/select_n | solution.py:387
Async XLA Ops:
  0.6 91.5 %copy-start = (f32[3,128,128]{2,1,0:T(8,128)S(1)}, f32[3,128,128]{2,1,0:T(8,128)}, u32[]{:S(2)}) copy-start(f32[3,128,128]{2,1,0:T(8,128)} %param.17) | copy-start | bytes 589828
  0.6 91.5 %copy-start.1 = (f32[3,128,128]{2,1,0:T(8,128)S(1)}, f32[3,128,128]{2,1,0:T(8,128)}, u32[]{:S(2)}) copy-start(f32[3,128,128]{2,1,0:T(8,128)} %param.15) | copy-start | bytes 589828
  0.7 91.5 %copy-start.2 = (f32[3,128,128]{2,1,0:T(8,128)S(1)}, f32[3,128,128]{2,1,0:T(8,128)}, u32[]{:S(2)}) copy-start(f32[3,128,128]{2,1,0:T(8,128)} %param.16) | copy-start | bytes 589828

commit v3 on v2

--- a/solution.py
+++ b/solution.py
@@ -23,7 +23,7 @@
 MESH = pl.DeviceIdType.MESH
 PARTS = 4
 ROWS = BS // PARTS
-LAG = 0
+ORDER = (0, 1, 2, 0, 3, 1, 2, 0, 3, 1, 2, 0, 3, 1, 2, 0, 3, 1, 2, 3)
 CHUNK = 4
 PER = CELLS // CHUNK
 RING = tuple(
@@ -159,17 +159,14 @@
     for k in range(HOPS - PER, HOPS):
         for way in (0, 1):
             ring(way, k, 1).wait_recv()
-    for k in range(HOPS):
-        for way in (0, 1):
-            ring(way, k, 0).wait_send()
 
     def product(xx, cc, i):
         k = table[0, i * 8 + xx * 2 + cc]
         a = acts[blk[0, k] * COLS + blk[2, k]]
         return jnp.dot(a, feats[blk[1, k]], preferred_element_type=F32)
 
-    def products(dst, n, xx, cc):
-        for i in range(8):
+    def products(dst, n, xx, cc, places=range(8)):
+        for i in places:
             dst[n, i] = product(xx, cc, i)
 
     rel = (2, 1, 3, 0)
@@ -178,14 +175,19 @@
     def send(*copy):
         c = rcopy(*copy)
         c.start()
-        sent.append(c)
         return c
 
     to_sib = {}
 
     def for_sib(n):
-        products(send_c, n, shift(x, rel[n], NX), 1 - core)
-        to_sib[n] = send(send_c.at[n], recv_c.at[n], cs.at[n], cr.at[n], sib)
+        xx = shift(x, rel[n], NX)
+        for m in (0, 1) if n == 0 else (0,):
+            places = slice(4 * m, 4 * m + 4) if n == 0 else slice(0, 8)
+            products(send_c, n, xx, 1 - core, range(8)[places])
+            part_c = pl.ds(places.start, places.stop - places.start)
+            to_sib[n, m] = send(
+                send_c.at[n, part_c], recv_c.at[n, part_c], cs.at[n, m], cr.at[n, m], sib
+            )
 
     def for_me(n):
         products(tot, n, shift(x, rel[n], NX), core)
@@ -200,26 +202,25 @@
         along_x[h][name] = send(src, dst, xs.at[h, n], xr.at[h, n], xdev[step])
 
     def core_sum(n):
-        to_sib[n].wait_recv()
-        tot[n] = tot[n] + recv_c[n]
-        for h in range(PARTS if n == 0 else 0):
-            if n == 0:
-                x_two[h] = tot[0, :, rows_of(h)].astype(BF16)
-                to_x(h, "two+", 0, x_two.at[h, lo], x_in.at[h, 0], 1)
-                to_x(h, "two-", 1, x_two.at[h, hi], x_in.at[h, 1], -1)
+        if n > 0:
+            to_sib[n, 0].wait_recv()
+            tot[n] = tot[n] + recv_c[n]
+            return
+        for m, (places, step) in enumerate(((lo, 1), (hi, -1))):
+            to_sib[0, m].wait_recv()
+            for h in range(PARTS):
+                x_two[h, places] = (tot[0, places, rows_of(h)] + recv_c[0, places, rows_of(h)]).astype(BF16)
+                to_x(h, ("two+", "two-")[m], m, x_two.at[h, places], x_in.at[h, m], step)
 
     for_sib(0)
     for_sib(1)
     for_me(0)
     core_sum(0)
+    for_sib(2)
     for_me(1)
-    for_sib(2)
     core_sum(1)
     for_me(2)
-    for_sib(3)
     core_sum(2)
-    for_me(3)
-    core_sum(3)
 
     col = x * 2 + core
 
@@ -236,6 +237,7 @@
         to_x(h, "one+", 2, x_one.at[h, 0], x_left.at[h, hi], 1)
         x_one[h, 1] = tot[2, lo, mine].astype(BF16)
         to_x(h, "one-", 3, x_one.at[h, 1], x_right.at[h, lo], -1)
+        yield
         moves["two+"].wait_recv()
         x_fwd[h, 0] = (tot[1, lo, mine] + x_in[h, 0].astype(F32)).astype(BF16)
         to_x(h, "fwd+", 4, x_fwd.at[h, 0], x_left.at[h, lo], 1)
@@ -267,15 +269,24 @@
         ways = (far, 1 - far)
         third = {w: along_y(w, 0, 3, 1) for w in ways}
         fourth = along_y(far, 2, 4, 2)
-        first = {w: along_y(w, 1, 1, 1) for w in ways}
-        yield
-        second = {}
+        yield
+        if h == 0:
+            for k in range(HOPS):
+                for way in (0, 1):
+                    ring(way, k, 0).wait_send()
+            for c in to_sib.values():
+                c.wait_send()
+        first, second = {}, {}
         for w in ways:
             third[w].wait_recv()
             if w == far:
                 fourth.wait_recv()
             second[w] = along_y(w, 3, 2, 2, (0, 2) if w == far else (0,))
-        yield
+        for w in ways:
+            first[w] = along_y(w, 1, 1, 1)
+        yield
+        for c in moves.values():
+            c.wait_send()
         for w in ways:
             first[w].wait_recv()
             second[w].wait_recv()
@@ -293,19 +304,24 @@
             x_copy[n].wait_recv()
             came = column(shift(x, -k, NX) * 2 + core, h)
             sib_copy.append(send(came, came, gs.at[h, 4 + n], gr.at[h, 4 + n], sib))
+        for c in (*third.values(), fourth, *first.values(), *second.values()):
+            c.wait_send()
         yield
         for c in sib_copy:
             c.wait_recv()
+        sent.extend((*x_copy, *sib_copy))
 
     turns = [tail(h) for h in range(PARTS)]
-    for turn in turns:
+    next(turns[0])
+    for_sib(3)
+    for_me(3)
+    next(turns[0])
+    for turn in turns[1:]:
         next(turn)
-    running, slot = set(range(PARTS)), 0
-    while running:
-        for h in sorted(running):
-            if h * LAG <= slot and next(turns[h], turns) is turns:
-                running.remove(h)
-        slot += 1
+        next(turn)
+    core_sum(3)
+    for h in ORDER:
+        next(turns[h], None)
 
     for s in range(CAP):
         q = mine_at[s]
@@ -358,8 +374,8 @@
             dma,
             dma((2, HOPS)),
             dma((2, HOPS)),
-            dma((4,)),
-            dma((4,)),
+            dma((4, 2)),
+            dma((4, 2)),
             dma((PARTS, 6)),
             dma((PARTS, 6)),
             dma((PARTS, 2, 4)),

time: 94.2 us -> 92.5 us (0.982)
  Pallas kernels: 90.8 us -> 89 us
    pallas_call x1, Pallas kernels: 90.8 us -> 89 us  [local(): pl.pallas_call(kernel, out_shape=(jax.ShapeDtypeStruct((CAP, BS, BS), F32...]
where the time goes in v3:
time: 92.5 us; the launch traced here: 92.3 us
  Pallas kernels  89 us (96%)
  other arithmetic  2.56 us (3%)
    pallas_call x1, Pallas kernels, local(): pl.pallas_call(kernel, out_shape=(jax.ShapeDtypeStruct((CAP, BS, BS), F32...  89 us
    select_n x1, other arithmetic, local(): jnp.where(is_valid, second_new, moment2)  1.92 us

profile of v3, /device:TPU:1, one launch (start us, length us, event | category | flops | bytes accessed | tf_op | source)
XLA Modules:
  0.0 92.3 jit_solution(4158023643507191336)
XLA Ops:
  0.6 0.0 copy-start
  0.6 0.0 copy-start.1
  0.7 0.0 copy-start.2
  0.7 89.0 %block_grads.1 = (f32[3,128,128]{2,1,0:T(8,128)}, s32[1]{0:T(128)}) custom-call(bf16[256,1024]{1,0:T(8,128)(2,1)} %feat.1, bf16[256,1792]{1,0:T(8,128)(2,1)} %gate.1, bf16[256,1792]{1,0:T(8,128)(2,1)} %up.1, bf16[256,1792]{1,0:T(8,128)(2,1)} %ghid.1, s32[3,64]{1,0:T(4,128)} %bitcast.3, s32[64]{0:T(128)} %own_s.1, s32[1,64]{1,0:T(1,128)} %bitcast.4), custom_call_target="tpu_custom_call" | custom-call | flops 536870912 | bytes 4194304 | tf_op jit(solution)/shard_map/block_grads/pallas_call | solution.py:343
  89.7 0.6 iota_compare_fusion
  90.3 0.0 copy-done
  90.4 0.0 copy-done.1
  90.4 0.0 copy-done.2
  90.4 1.9 %fusion.2 = (f32[3,128,128]{2,1,0:T(8,128)}, f32[3,128,128]{2,1,0:T(8,128)}, f32[3,128,128]{2,1,0:T(8,128)}) fusion(f32[3,128,128]{2,1,0:T(8,128)S(1)} %copy-done, f32[3,128,128]{2,1,0:T(8,128)} %get-tuple-element.6, pred[3]{0:T(512)(128)(4,1)S(1)} %iota_compare_fusion, f32[3,128,128]{2,1,0:T(8,128)S(1)} %copy-done.1, f32[3,128,128]{2,1,0:T(8,128)S(1)} %copy-done.2), kind=kLoop, calls=%fused_computation.5 | loop fusion | flops 737280 | bytes 1376259 | tf_op jit(solution)/shard_map/jit(_where)/select_n | solution.py:403
Async XLA Ops:
  0.6 89.7 %copy-start = (f32[3,128,128]{2,1,0:T(8,128)S(1)}, f32[3,128,128]{2,1,0:T(8,128)}, u32[]{:S(2)}) copy-start(f32[3,128,128]{2,1,0:T(8,128)} %param.17) | copy-start | bytes 589828
  0.6 89.7 %copy-start.1 = (f32[3,128,128]{2,1,0:T(8,128)S(1)}, f32[3,128,128]{2,1,0:T(8,128)}, u32[]{:S(2)}) copy-start(f32[3,128,128]{2,1,0:T(8,128)} %param.15) | copy-start | bytes 589828
  0.7 89.7 %copy-start.2 = (f32[3,128,128]{2,1,0:T(8,128)S(1)}, f32[3,128,128]{2,1,0:T(8,128)}, u32[]{:S(2)}) copy-start(f32[3,128,128]{2,1,0:T(8,128)} %param.16) | copy-start | bytes 589828

commit v4 on v3

--- a/solution.py
+++ b/solution.py
@@ -384,7 +384,7 @@
             dma((PARTS, 7)),
         ],
         compiler_params=pltpu.CompilerParams(
-            collective_id=0, has_side_effects=True, vmem_limit_bytes=60 * 2**20
+            collective_id=0, has_side_effects=True, vmem_limit_bytes=107 * 2**19
         ),
         cost_estimate=pl.CostEstimate(
             flops=2 * LISTED * tokens * BS * BS, bytes_accessed=4 * 2**20, transcendentals=tokens * COLS * BS

time: 92.5 us -> 91.9 us (level)
  no operation moved by 1% of the time
where the time goes in v4:
time: 91.9 us; the launch traced here: 91.8 us
  Pallas kernels  88.7 us (97%)
  other arithmetic  1.7 us (2%)
    pallas_call x1, Pallas kernels, local(): pl.pallas_call(kernel, out_shape=(jax.ShapeDtypeStruct((CAP, BS, BS), F32...  88.7 us

profile of v4, /device:TPU:1, one launch (start us, length us, event | category | flops | bytes accessed | tf_op | source)
XLA Modules:
  0.0 91.8 jit_solution(3292534453560767359)
XLA Ops:
  0.6 0.0 copy-start
  0.6 0.0 copy-start.1
  0.7 0.7 copy-done
  1.3 0.0 copy-done.1
  1.3 0.0 copy-start.2
  1.3 0.0 copy-start.3
  1.3 0.0 copy-start.4
  1.3 88.7 %block_grads.1 = (f32[3,128,128]{2,1,0:T(8,128)S(1)}, s32[1]{0:T(128)}) custom-call(bf16[256,1024]{1,0:T(8,128)(2,1)} %feat.1, bf16[256,1792]{1,0:T(8,128)(2,1)} %gate.1, bf16[256,1792]{1,0:T(8,128)(2,1)} %up.1, bf16[256,1792]{1,0:T(8,128)(2,1)} %ghid.1, s32[3,64]{1,0:T(4,128)S(1)} %bitcast.3, s32[64]{0:T(128)S(1)} %copy-done.1, s32[1,64]{1,0:T(1,128)S(1)} %bitcast.4), custom_call_target="tpu_custom_call" | custom-call | flops 536870912 | bytes 4194304 | tf_op jit(solution)/shard_map/block_grads/pallas_call | solution.py:343
  90.0 0.7 iota_compare_fusion
  90.7 0.0 copy-done.2
  90.8 0.0 copy-done.3
  90.8 0.0 copy-done.4
  90.8 1.0 %fusion.2 = (f32[3,128,128]{2,1,0:T(8,128)}, f32[3,128,128]{2,1,0:T(8,128)}, f32[3,128,128]{2,1,0:T(8,128)}) fusion(f32[3,128,128]{2,1,0:T(8,128)S(1)} %copy-done.2, f32[3,128,128]{2,1,0:T(8,128)S(1)} %get-tuple-element.6, pred[3]{0:T(512)(128)(4,1)S(1)} %iota_compare_fusion, f32[3,128,128]{2,1,0:T(8,128)S(1)} %copy-done.3, f32[3,128,128]{2,1,0:T(8,128)S(1)} %copy-done.4), kind=kLoop, calls=%fused_computation.5 | loop fusion | flops 737280 | bytes 1376259 | tf_op jit(solution)/shard_map/jit(_where)/select_n | solution.py:403
Async XLA Ops:
  0.6 0.7 copy-start
  0.6 0.7 copy-start.1
  1.3 89.4 %copy-start.2 = (f32[3,128,128]{2,1,0:T(8,128)S(1)}, f32[3,128,128]{2,1,0:T(8,128)}, u32[]{:S(2)}) copy-start(f32[3,128,128]{2,1,0:T(8,128)} %param.17) | copy-start | bytes 589828
  1.3 89.4 %copy-start.3 = (f32[3,128,128]{2,1,0:T(8,128)S(1)}, f32[3,128,128]{2,1,0:T(8,128)}, u32[]{:S(2)}) copy-start(f32[3,128,128]{2,1,0:T(8,128)} %param.15) | copy-start | bytes 589828
  1.3 89.4 %copy-start.4 = (f32[3,128,128]{2,1,0:T(8,128)S(1)}, f32[3,128,128]{2,1,0:T(8,128)}, u32[]{:S(2)}) copy-start(f32[3,128,128]{2,1,0:T(8,128)} %param.16) | copy-start | bytes 589828
